TPU v7x, 32 devices: a whole 2x2x4 slice. The times are simulated.
32 devices in a mesh: groups: 2 (over y), role: 4 (over x, core), tp: 4 (over z).
Axes of the slice: x: 2, y: 2, z: 4, core: 2. Of those that a mesh axis runs over, the one named last changes fastest.
Arguments:
- x_teacher: bfloat16 [512, 8192], P('groups', 'tp'), parts along dimension 0, may hold values from -6 to 6
- x_student: bfloat16 [512, 4096], P('groups', 'role'), parts along dimension 0, may hold values from -6 to 6
- t_gate: bfloat16 [8192, 14336], P('tp', 'role'), may hold values from -0.0625 to 0.0625
- t_up: bfloat16 [8192, 14336], P('tp', 'role'), may hold values from -0.0625 to 0.0625
- t_down: bfloat16 [14336, 8192], P('role', 'tp'), may hold values from -0.046875 to 0.046875
- s_gate: bfloat16 [4096, 8192], P('role', 'tp'), may hold values from -0.09375 to 0.09375
- s_up: bfloat16 [4096, 8192], P('role', 'tp'), may hold values from -0.09375 to 0.09375
- s_down: bfloat16 [8192, 4096], P('tp', 'role'), may hold values from -0.0625 to 0.0625
- align: bfloat16 [4096, 8192], P('role', 'tp'), may hold values from -0.09375 to 0.09375
Outputs:
- grad_s_gate: bfloat16 [8192, 8192], P(('groups', 'role'), 'tp'), parts along dimension 0
- grad_s_up: bfloat16 [8192, 8192], P(('groups', 'role'), 'tp'), parts along dimension 0
- grad_s_down: bfloat16 [16384, 4096], P(('groups', 'tp'), 'role'), parts along dimension 0
- grad_align: bfloat16 [8192, 8192], P(('groups', 'role'), 'tp'), parts along dimension 0
There are 2 independent parts, one for each index of `groups`. A program takes and returns all parts, laid end to end along the dimension named above; an argument that names none is the same for every part. Nothing has to cross between parts.
All inputs are finite; a program needn't handle non-finite values.
Results may differ from a plain program's by a relative error of at most 0.009.
Values may be sent and summed in bfloat16 or wider, within the bound.
A program may use at most 128 MiB of HBM per device.

v0:
```python
import jax
import jax.numpy as jnp
from jax import lax
from jax.sharding import PartitionSpec as P

loss_scale = 16.0


def contract_rows(left, right):
    return lax.dot_general(
        left, right, (((0,), (0,)), ((), ())), preferred_element_type=jnp.float32
    )


def contract_cols(left, right):
    return lax.dot_general(
        left, right, (((1,), (1,)), ((), ())), preferred_element_type=jnp.float32
    )


def role_sums(values):
    return lax.psum(values, "role")


def tp_sums(values):
    return lax.psum(values, "tp")


def tp_scatter(term_fn, share_rows):
    return lax.psum_scatter(
        term_fn(jnp.int32(0), lax.axis_size("tp") * share_rows),
        "tp",
        scatter_dimension=0,
        tiled=True,
    )


def tp_gather(shares, piece_fn):
    return piece_fn(lax.all_gather(shares, "tp", axis=0, tiled=True), jnp.int32(0))


def on_device(x_teacher, x_student, t_gate, t_up, t_down, s_gate, s_up, s_down, align):
    token_count = x_teacher.shape[0]
    unit_count = t_gate.shape[1]
    tp_devices = lax.axis_size("tp")

    def token_term(first_row, row_count):
        gate_rows = jnp.dot(x_teacher, t_gate, preferred_element_type=jnp.float32)
        up_rows = jnp.dot(x_teacher, t_up, preferred_element_type=jnp.float32)
        return jnp.concatenate([gate_rows, up_rows], axis=1)

    def project_rows(part_rows, first_row):
        return jnp.dot(part_rows, t_down, preferred_element_type=jnp.float32)

    shares = tp_scatter(token_term, token_count // tp_devices)
    hidden_share = (jax.nn.silu(shares[:, :unit_count]) * shares[:, unit_count:]).astype(
        jnp.bfloat16
    )
    features_part = tp_gather(hidden_share, project_rows)
    student_gate_part = jnp.dot(x_student, s_gate, preferred_element_type=jnp.float32)
    student_up_part = jnp.dot(x_student, s_up, preferred_element_type=jnp.float32)
    student_gate, student_up = role_sums((student_gate_part, student_up_part))
    gate_sigmoid = jax.nn.sigmoid(student_gate)
    gate_active = student_gate * gate_sigmoid
    student_hidden = (gate_active * student_up).astype(jnp.bfloat16)
    student_out = tp_sums(
        jnp.dot(student_hidden, s_down, preferred_element_type=jnp.float32)
    ).astype(jnp.bfloat16)
    aligned_part = jnp.dot(student_out, align, preferred_element_type=jnp.float32)
    difference = role_sums(aligned_part - features_part)
    grad_aligned = (difference * (2.0 * loss_scale / token_count)).astype(jnp.bfloat16)
    grad_align = contract_rows(student_out, grad_aligned).astype(jnp.bfloat16)
    grad_student_out = tp_sums(contract_cols(grad_aligned, align)).astype(jnp.bfloat16)
    grad_s_down = contract_rows(student_hidden, grad_student_out).astype(jnp.bfloat16)
    grad_hidden = role_sums(contract_cols(grad_student_out, s_down))
    slope = gate_sigmoid * (1.0 + student_gate * (1.0 - gate_sigmoid))
    grad_gate_pre = (grad_hidden * student_up * slope).astype(jnp.bfloat16)
    grad_up_pre = (grad_hidden * gate_active).astype(jnp.bfloat16)
    grad_s_gate = contract_rows(x_student, grad_gate_pre).astype(jnp.bfloat16)
    grad_s_up = contract_rows(x_student, grad_up_pre).astype(jnp.bfloat16)
    return (grad_s_gate, grad_s_up, grad_s_down, grad_align)


def solution(mesh):
    placed = (
        P("groups", "tp"),
        P("groups", "role"),
        P("tp", "role"),
        P("tp", "role"),
        P("role", "tp"),
        P("role", "tp"),
        P("role", "tp"),
        P("tp", "role"),
        P("role", "tp"),
    )
    return jax.shard_map(
        on_device,
        mesh=mesh,
        in_specs=placed,
        out_specs=(
            P(("groups", "role"), "tp"),
            P(("groups", "role"), "tp"),
            P(("groups", "tp"), "role"),
            P(("groups", "role"), "tp"),
        ),
        check_vma=False,
    )
```

profile of v0, /device:TPU:0, one launch (start us, length us, event | category | flops | bytes accessed | tf_op | source)
XLA Modules:
  0.0 431.8 jit_solution(6002679710210174196)
XLA Ops:
  8.0 0.0 reduce-scatter.2.cloned.1.call-start
  8.1 1.2 copy-done
  9.2 7.2 %fusion.18 = f32[256,3584]{1,0:T(8,128)S(1)} fusion(bf16[256,2048]{1,0:T(8,128)(2,1)S(1)} %copy-done, bf16[2048,3584]{1,0:T(8,128)(2,1)} %param.12), kind=kOutput, calls=%fused_computation.29 | convolution fusion | flops 3758096384 | bytes 19398656 | tf_op jit(solution)/shard_map/dot_general | solution.py:49
  16.5 7.3 %fusion.17 = f32[256,3584]{1,0:T(8,128)S(1)} fusion(bf16[256,2048]{1,0:T(8,128)(2,1)S(1)} %copy-done, bf16[2048,3584]{1,0:T(8,128)(2,1)} %param.11), kind=kOutput, calls=%fused_computation.28 | convolution fusion | flops 3758096384 | bytes 19398656 | tf_op jit(solution)/shard_map/dot_general | solution.py:48
  23.8 3.4 pad_maximum_fusion
  27.3 0.0 all-reduce.11.cloned.1.call-start
  27.3 1.0 copy-done.7
  28.3 4.9 %fusion.14 = f32[256,2048]{1,0:T(8,128)} fusion(bf16[256,1024]{1,0:T(8,128)(2,1)S(1)} %copy-done.7, bf16[1024,2048]{1,0:T(8,128)(2,1)} %param.14), kind=kOutput, calls=%fused_computation.25 | convolution fusion | flops 1073741824 | bytes 6815744 | tf_op jit(solution)/shard_map/dot_general | solution.py:60
  33.2 2.6 fusion.15
  35.8 0.0 all-gather.2.cloned.1.call-start
  35.9 122.0 %reduce-scatter.2.cloned.1.call-done = f32[64,7168]{1,0:T(8,128)} async-done(((f32[256,7168]{1,0:T(8,128)}), f32[64,7168]{1,0:T(8,128)}) %reduce-scatter.2.cloned.1.call-update) | async-done | bytes 1835024 | tf_op jit(solution)/shard_map/reduce_scatter | solution.py:30
  157.9 2.5 fusion.2
  160.4 0.0 all-reduce.7.cloned.1.call-start
  160.4 0.0 all-reduce.11.cloned.1.call-done
  160.5 3.0 multiply_convert_fusion.3
  163.5 0.5 copy-done.6
  163.9 1.3 fusion.16
  165.2 70.1 %all-reduce.12 = bf16[256,1024]{1,0:T(8,128)(2,1)S(1)} all-reduce(f32[256,1024]{1,0:T(8,128)S(1)} %fusion.16), channel_id=1, replica_groups=mesh['groups'=2,'role'=4,'tp'=4] {'tp'}, use_global_device_ids=true, to_apply=%region_2.3 | all-reduce | flops 262144 | bytes 1572864 | tf_op jit(solution)/shard_map/psum | solution.py:26
  235.3 7.9 %fusion.19 = f32[256,2048]{1,0:T(8,128)S(1)} fusion(bf16[256,3584]{1,0:T(8,128)(2,1)} %all-gather.2.cloned.1.call-done, bf16[3584,2048]{1,0:T(8,128)(2,1)} %param.13), kind=kOutput, calls=%fused_computation.30 | convolution fusion | flops 3758096384 | bytes 18612224 | tf_op jit(solution)/shard_map/dot_general | solution.py:53
  243.3 2.6 convolution_subtract_fusion
  245.9 0.2 all-reduce.9.cloned.1.call-start
  246.1 50.9 %all-reduce.7.cloned.1.call-done = f32[256,2048]{1,0:T(8,128)} async-done(((f32[256,2048]{1,0:T(8,128)}), f32[256,2048]{1,0:T(8,128)}) %all-reduce.7.cloned.1.call-update) | async-done | bytes 2097168 | tf_op jit(solution)/shard_map/psum | solution.py:22
  297.0 4.1 fusion.3
  301.1 43.7 %all-reduce.13 = bf16[256,1024]{1,0:T(8,128)(2,1)S(1)} all-reduce(f32[256,1024]{1,0:T(8,128)S(1)} %fusion.3), channel_id=1, replica_groups=mesh['groups'=2,'role'=4,'tp'=4] {'tp'}, use_global_device_ids=true, to_apply=%region_5.6 | all-reduce | flops 262144 | bytes 1572864 | tf_op jit(solution)/shard_map/psum | solution.py:26
  344.8 4.8 %fusion.20 = f32[256,2048]{1,0:T(8,128)} fusion(bf16[256,1024]{1,0:T(8,128)(2,1)S(1)} %all-reduce.13, bf16[2048,1024]{1,0:T(8,128)(2,1)} %param.16), kind=kOutput, calls=%fused_computation.31 | convolution fusion | flops 1073741824 | bytes 6815744 | tf_op jit(solution)/shard_map/dot_general | solution.py:16
  349.6 3.3 convolution_convert_fusion.1
  352.9 3.3 convolution_convert_fusion
  356.2 43.0 %all-reduce.9.cloned.1.call-done = f32[256,2048]{1,0:T(8,128)} async-done(((f32[256,2048]{1,0:T(8,128)}), f32[256,2048]{1,0:T(8,128)}) %all-reduce.9.cloned.1.call-update) | async-done | bytes 2097168 | tf_op jit(solution)/shard_map/psum | solution.py:22
  399.2 7.0 %convert_bitcast_fusion.1 = bf16[1024,2048]{0,1:T(8,128)(2,1)} fusion(bf16[256,1024]{1,0:T(8,128)(2,1)S(1)} %copy-done.8, f32[256,2048]{1,0:T(8,128)} %get-tuple-element.8, f32[256,2048]{1,0:T(8,128)} %all-reduce.9.cloned.1.call-done, f32[256,2048]{1,0:T(8,128)} %get-tuple-element.9), kind=kOutput, calls=%fused_computation.2 | convolution fusion | flops 1081081856 | bytes 11010048 | tf_op jit(solution)/shard_map/dot_general | solution.py:10
  406.2 6.6 %copy.13 = bf16[1024,2048]{1,0:T(8,128)(2,1)} copy(bf16[1024,2048]{0,1:T(8,128)(2,1)} %convert_bitcast_fusion.1) | data formatting | bytes 8388608
  412.8 4.9 %convert_bitcast_fusion = bf16[1024,2048]{0,1:T(8,128)(2,1)} fusion(bf16[256,1024]{1,0:T(8,128)(2,1)S(1)} %copy-done.8, f32[256,2048]{1,0:T(8,128)} %all-reduce.9.cloned.1.call-done, f32[256,2048]{1,0:T(8,128)S(1)} %copy-done.4), kind=kOutput, calls=%fused_computation.1 | convolution fusion | flops 1078984704 | bytes 8912896 | tf_op jit(solution)/shard_map/dot_general | solution.py:10
  417.7 6.5 %copy.14 = bf16[1024,2048]{1,0:T(8,128)(2,1)} copy(bf16[1024,2048]{0,1:T(8,128)(2,1)} %convert_bitcast_fusion) | data formatting | bytes 8388608
  (21 shorter events, 0.1 us)
Async XLA Ops:
  8.0 1.2 copy-start
  8.0 149.9 %reduce-scatter.2.cloned.1.call-start = ((), (), s32[]{:S(2)}) async-start(), calls=%async_computation.1 | async-start | bytes 9175040 | tf_op jit(solution)/shard_map/reduce_scatter | solution.py:30
  27.2 1.0 copy-start.7
  27.3 133.2 %all-reduce.11.cloned.1.call-start = ((), (), s32[]{:S(2)}) async-start(), calls=%async_computation.5 | async-start | bytes 8388608 | tf_op jit(solution)/shard_map/psum | solution.py:22
  28.3 4.9 %copy-start.5 = (bf16[1024,2048]{1,0:T(8,128)(2,1)S(1)}, bf16[1024,2048]{1,0:T(8,128)(2,1)}, u32[]{:S(2)}) copy-start(bf16[1024,2048]{1,0:T(8,128)(2,1)} %param.15) | copy-start | bytes 12582916
  35.8 199.5 %all-gather.2.cloned.1.call-start = ((), (), s32[]{:S(2)}) async-start(), calls=%async_computation.2 | async-start | bytes 2293760 | tf_op jit(solution)/shard_map/all_gather | solution.py:39
  160.4 136.6 %all-reduce.7.cloned.1.call-start = ((), (), s32[]{:S(2)}) async-start(), calls=%async_computation.3 | async-start | bytes 4194304 | tf_op jit(solution)/shard_map/psum | solution.py:22
  160.5 3.5 copy-start.6
  235.3 8.0 %copy-start.2 = (bf16[1024,2048]{1,0:T(8,128)(2,1)S(1)}, bf16[1024,2048]{1,0:T(8,128)(2,1)}, u32[]{:S(2)}) copy-start(bf16[1024,2048]{1,0:T(8,128)(2,1)} %param.17) | copy-start | bytes 12582916
  245.9 153.3 %all-reduce.9.cloned.1.call-start = ((), (), s32[]{:S(2)}) async-start(), calls=%async_computation.4 | async-start | bytes 4194304 | tf_op jit(solution)/shard_map/psum | solution.py:22
  349.6 3.3 copy-start.3
  352.9 46.3 %copy-start.8 = (bf16[256,1024]{1,0:T(8,128)(2,1)S(1)}, bf16[256,1024]{1,0:T(8,128)(2,1)}, u32[]{:S(2)}) copy-start(bf16[256,1024]{1,0:T(8,128)(2,1)} %param.10) | copy-start | bytes 1572868
  406.2 6.6 %copy-start.4 = (f32[256,2048]{1,0:T(8,128)S(1)}, f32[256,2048]{1,0:T(8,128)}, u32[]{:S(2)}) copy-start(f32[256,2048]{1,0:T(8,128)} %get-tuple-element.8) | copy-start | bytes 6291460
  417.7 6.5 %copy-start.1 = (bf16[256,2048]{1,0:T(8,128)(2,1)S(1)}, bf16[256,2048]{1,0:T(8,128)(2,1)}, u32[]{:S(2)}) copy-start(bf16[256,2048]{1,0:T(8,128)(2,1)} %param.9) | copy-start | bytes 3145732
Sparse Core Ops, SparseCore 0:
  27.4 130.4 reduce-scatter.1
  160.5 69.8 all-gather.1
Sparse Core Ops, SparseCore 1:
  35.9 88.2 all-reduce.10
  246.0 50.9 all-reduce.6
  349.7 49.5 all-reduce.8
where the time goes:
time: 432 us
  waiting for transfers between devices  216 us (50%)
  blocking collectives  114 us (26%)
  matrix products  61.3 us (14%)
  between operations  15.8 us (4%)
  local copies, waits for them, and re-layouts  15.7 us (4%)
  other arithmetic  8.9 us (2%)
    reduce_scatter x1, waiting for transfers between devices, tp_scatter(): lax.psum_scatter(term_fn(jnp.int32(0), lax.axis_size('tp') * share_rows),...  122 us
    psum x2, blocking collectives, tp_sums(): return lax.psum(values, 'tp')  114 us
    psum x3, waiting for transfers between devices, role_sums(): return lax.psum(values, 'role')  93.8 us
    dot_general x4, matrix products, contract_rows(): lax.dot_general(left, right, (((0,), (0,)), ((), ())), preferred_element_...  18.5 us
    unnamed x20, local copies, waits for them, and re-layouts  15.7 us
    dot_general x2, matrix products, contract_cols(): lax.dot_general(left, right, (((1,), (1,)), ((), ())), preferred_element_...  8.9 us
  transfers between devices with their start and end apart: 5, of which 3 were waited for; matrix products, arithmetic and copies ran while one was open for 5% of the time, Pallas kernels for 0%

commit v1 on v0

v1 whole, which is shorter than its diff:
```python
import functools

import jax
import jax.numpy as jnp
from jax import lax
from jax.experimental import pallas as pl
from jax.experimental.pallas import tpu as pltpu
from jax.sharding import PartitionSpec as P

loss_scale = 16.0
MESH = pl.DeviceIdType.MESH
BF16 = jnp.bfloat16
F32 = jnp.float32
SKEW = 2
TEACHER_SLOTS = 3
DOWN_SLOTS = 3
PIECES = 4


def width_of(columns, wanted):
    width = wanted
    while columns % width:
        width //= 2
    return width


def sum_scratch(devices, half, columns, first_type, finals):
    peers = devices // 2 - 1
    return dict(
        sent1=pltpu.VMEM((half, columns), first_type),
        got1=pltpu.VMEM((half, columns), first_type),
        sent2=pltpu.VMEM((half, columns), BF16),
        got2=pltpu.VMEM((peers, half, columns), BF16),
        s1=pltpu.SemaphoreType.DMA((PIECES,)),
        r1=pltpu.SemaphoreType.DMA((PIECES,)),
        s2=pltpu.SemaphoreType.DMA((peers, PIECES)),
        r2=pltpu.SemaphoreType.DMA((peers, PIECES)),
        s3=pltpu.SemaphoreType.DMA((finals, PIECES)),
        r3=pltpu.SemaphoreType.DMA((finals, PIECES)),
    )


class Summed:
    def __init__(self, axis, part, columns, bufs, finals, finish):
        self.axis = axis
        self.count = lax.axis_size(axis)
        self.me = lax.axis_index(axis)
        self.own = lax.rem(self.me, 2)
        self.pair = self.me + 1 - 2 * self.own
        self.part, self.columns, self.b = part, columns, bufs
        self.finals, self.finish = finals, finish
        self.half = part.shape[1]
        self.step = self.half // PIECES
        self.tile = width_of(columns, 1024)

    def rows(self, k):
        return pl.ds(k * self.step, self.step)

    def tiles(self):
        return [pl.ds(j, self.tile) for j in range(0, self.columns, self.tile)]

    def copy1(self, k):
        rows = self.rows(k)
        return pltpu.make_async_remote_copy(
            src_ref=self.b["sent1"].at[rows], dst_ref=self.b["got1"].at[rows],
            send_sem=self.b["s1"].at[k], recv_sem=self.b["r1"].at[k],
            device_id={self.axis: self.pair}, device_id_type=MESH)

    def copy2(self, j, k):
        rows = self.rows(k)
        return pltpu.make_async_remote_copy(
            src_ref=self.b["sent2"].at[rows], dst_ref=self.b["got2"].at[j, rows],
            send_sem=self.b["s2"].at[j, k], recv_sem=self.b["r2"].at[j, k],
            device_id={self.axis: lax.rem(self.me + 2 * (j + 1), self.count)},
            device_id_type=MESH)

    def copy3(self, i, k, owner):
        rows = self.rows(k)
        ref = self.finals[i].at[owner, rows]
        return pltpu.make_async_remote_copy(
            src_ref=ref, dst_ref=ref,
            send_sem=self.b["s3"].at[i, k], recv_sem=self.b["r3"].at[i, k],
            device_id={self.axis: self.pair}, device_id_type=MESH)

    def phase1(self):
        for k in range(PIECES):
            rows = self.rows(k)
            for cols in self.tiles():
                self.b["sent1"][rows, cols] = self.part[1 - self.own, rows, cols].astype(
                    self.b["sent1"].dtype)
            self.copy1(k).start()

    def phase2(self):
        for k in range(PIECES):
            rows = self.rows(k)
            self.copy1(k).wait_recv()
            for cols in self.tiles():
                total = self.part[self.own, rows, cols] + self.b["got1"][rows, cols].astype(F32)
                self.part[self.own, rows, cols] = total
                self.b["sent2"][rows, cols] = total.astype(BF16)
            for j in range(self.count // 2 - 1):
                self.copy2(j, k).start()

    def phase3(self):
        for k in range(PIECES):
            rows = self.rows(k)
            for j in range(self.count // 2 - 1):
                self.copy2(j, k).wait_recv()
            for cols in self.tiles():
                total = self.part[self.own, rows, cols]
                for j in range(self.count // 2 - 1):
                    total = total + self.b["got2"][j, rows, cols].astype(F32)
                self.part[self.own, rows, cols] = total
            self.finish(self.own, rows)
            for i in range(len(self.finals)):
                self.copy3(i, k, self.own).start()

    def phase4(self):
        for k in range(PIECES):
            for i in range(len(self.finals)):
                self.copy3(i, k, 1 - self.own).wait_recv()

    def drain(self):
        for k in range(PIECES):
            self.copy1(k).wait_send()
            for j in range(self.count // 2 - 1):
                self.copy2(j, k).wait_send()
            for i in range(len(self.finals)):
                self.copy3(i, k, self.own).wait_send()


def whole(ref):
    return ref[...].reshape(ref.shape[0] * ref.shape[1], ref.shape[2])


def exchange_kernel(names, chunk, x_t, x_s, tg, tu, td, sg, su, sd, al,
                    o_so, o_ga, o_sh, o_gso, o_gg, o_gu, *scratch):
    s = jax.tree.unflatten(names, scratch)
    tp, role = lax.axis_size("tp"), lax.axis_size("role")
    me, my_role = lax.axis_index("tp"), lax.axis_index("role")
    tokens = x_t.shape[0]
    half = tokens // 2
    units = tg.shape[1]
    chunks = units // chunk
    student_units = sg.shape[1]
    held = s["sums"].shape[0]
    last = tp - 1

    def teacher_load(c):
        cols = pl.ds(pl.multiple_of(c * chunk, chunk), chunk)
        slot = lax.rem(c, TEACHER_SLOTS)
        return (
            pltpu.make_async_copy(tg.at[:, cols], s["t_slot"].at[slot, 0], s["t_sem"].at[slot, 0]),
            pltpu.make_async_copy(tu.at[:, cols], s["t_slot"].at[slot, 1], s["t_sem"].at[slot, 1]),
        )

    def down_load(c):
        slot = lax.rem(c, DOWN_SLOTS)
        return pltpu.make_async_copy(
            td.at[pl.ds(pl.multiple_of(c * chunk, chunk), chunk)],
            s["d_slot"].at[slot], s["d_sem"].at[slot])

    load_sg = pltpu.make_async_copy(sg, s["w_gate"], s["w_sem"].at[0])
    load_su = pltpu.make_async_copy(su, s["w_gate"], s["w_sem"].at[1])
    load_sd = pltpu.make_async_copy(sd, s["w_down"], s["w_sem"].at[2])
    load_al = pltpu.make_async_copy(al, s["w_align"], s["w_sem"].at[3])

    for c in range(min(TEACHER_SLOTS, chunks)):
        for load in teacher_load(c):
            load.start()
    load_sg.start()
    load_sd.start()
    load_al.start()
    for c in range(min(DOWN_SLOTS, chunks)):
        down_load(c).start()

    barrier = pltpu.get_barrier_semaphore()
    for other in range(1, tp):
        pl.semaphore_signal(barrier, inc=1, device_id={"tp": lax.rem(me + other, tp)},
                            device_id_type=MESH)
    for other in range(1, role):
        pl.semaphore_signal(barrier, inc=1, device_id={"role": lax.rem(my_role + other, role)},
                            device_id_type=MESH)
    pl.semaphore_wait(barrier, tp + role - 2)

    s["diff"][...] = jnp.zeros_like(s["diff"])

    def rs_copy(way, c, target):
        ref = s["run"].at[way, c]
        return pltpu.make_async_remote_copy(
            src_ref=ref, dst_ref=ref, send_sem=s["run_s"].at[way, c],
            recv_sem=s["run_r"].at[way, c], device_id={"tp": target}, device_id_type=MESH)

    def ag_copy(way, c, target):
        ref = s["hid"].at[c, way]
        return pltpu.make_async_remote_copy(
            src_ref=ref, dst_ref=ref, send_sem=s["hid_s"].at[way, c],
            recv_sem=s["hid_r"].at[way, c], device_id={"tp": target}, device_id_type=MESH)

    def finish_hidden(own, rows):
        tile = width_of(student_units, 1024)
        for j in range(0, student_units, tile):
            gate = s["gate_up"][own, rows, pl.ds(j, tile)]
            up = s["gate_up"][own, rows, pl.ds(student_units + j, tile)]
            s["sh"][own, rows, pl.ds(j, tile)] = (gate * jax.nn.sigmoid(gate) * up).astype(BF16)

    def finish_out(own, rows):
        s["so"][own, rows] = s["narrow"][own, rows].astype(BF16)

    def finish_diff(own, rows):
        s["ga"][own, rows] = (s["diff"][own, rows] * (2.0 * loss_scale / tokens)).astype(BF16)

    def finish_grad_out(own, rows):
        s["gso"][own, rows] = s["narrow"][own, rows].astype(BF16)

    def finish_grad_hidden(own, rows):
        tile = width_of(student_units, 1024)
        for j in range(0, student_units, tile):
            gate = s["gate_up"][own, rows, pl.ds(j, tile)]
            up = s["gate_up"][own, rows, pl.ds(student_units + j, tile)]
            grad = s["diff"][own, rows, pl.ds(j, tile)]
            sigmoid = jax.nn.sigmoid(gate)
            slope = sigmoid * (1.0 + gate * (1.0 - sigmoid))
            s["gg"][own, rows, pl.ds(j, tile)] = (grad * up * slope).astype(BF16)
            s["gu"][own, rows, pl.ds(j, tile)] = (grad * (gate * sigmoid)).astype(BF16)

    wide, narrow = sg.shape[1], sd.shape[1]
    sum_gate = Summed("role", s["gate_up"], 2 * student_units, s["b_gate"], [s["sh"]], finish_hidden)
    sum_out = Summed("tp", s["narrow"], narrow, s["b_out"], [s["so"]], finish_out)
    sum_diff = Summed("role", s["diff"], al.shape[1], s["b_diff"], [s["ga"]], finish_diff)
    sum_grad = Summed("tp", s["narrow"], narrow, s["b_grad"], [s["gso"]], finish_grad_out)
    sum_hidden = Summed("role", s["diff"], wide, s["b_hidden"], [s["gg"], s["gu"]],
                        finish_grad_hidden)

    def product(left, right, out, first_col, columns, transposed, add):
        tile = width_of(columns, 256)

        @pl.loop(0, columns // tile)
        def _(j):
            at = pl.multiple_of(j * tile, tile)
            if transposed:
                block = lax.dot_general(left, right[pl.ds(at, tile)], (((1,), (1,)), ((), ())),
                                        preferred_element_type=F32)
            else:
                block = jnp.dot(left, right[:, pl.ds(at, tile)], preferred_element_type=F32)
            block = block.reshape(2, half, tile)
            cols = pl.ds(pl.multiple_of(first_col + at, tile), tile)
            if add:
                out[:, :, cols] = out[:, :, cols] + block
            else:
                out[:, :, cols] = block

    def student_gate():
        load_sg.wait()
        product(x_s[...], s["w_gate"], s["gate_up"], 0, student_units, False, False)
        load_su.start()

    def student_up():
        load_su.wait()
        product(x_s[...], s["w_gate"], s["gate_up"], student_units, student_units, False, False)
        sum_gate.phase1()

    def student_down():
        sum_gate.phase4()
        load_sd.wait()
        product(whole(s["sh"]), s["w_down"], s["narrow"], 0, narrow, False, False)
        sum_out.phase1()

    def student_align():
        sum_out.phase4()
        load_al.wait()
        product(whole(s["so"]), s["w_align"], s["diff"], 0, al.shape[1], False, True)

    steps = max(chunks + 2 * SKEW * last, 18)
    plan = [student_gate, student_up, sum_gate.phase2, sum_gate.phase3, student_down,
            sum_out.phase2, sum_out.phase3, student_align]
    wanted = [1, 2, 3, 9, 10, 12, 15, 17]

    @pl.loop(0, steps)
    def _(t):
        @pl.when(t < chunks)
        def _():
            for load in teacher_load(t):
                load.wait()
            slot = lax.rem(t, TEACHER_SLOTS)
            for k in range(2):
                block = jnp.dot(x_t[...], s["t_slot"][slot, k], preferred_element_type=F32)
                s["sums"][lax.rem(t, held), :, :, k * chunk:(k + 1) * chunk] = block.reshape(
                    2, half, chunk)

            @pl.when(t + TEACHER_SLOTS < chunks)
            def _():
                for load in teacher_load(t + TEACHER_SLOTS):
                    load.start()

        for way in range(2):
            hop = last - me if way == 0 else me
            onward = lax.rem(me + (tp - 1 if way == 0 else 1), tp)
            back = lax.rem(me + (1 if way == 0 else tp - 1), tp)
            c = t - SKEW * hop

            @pl.when((c >= 0) & (c < chunks))
            def _():
                at = lax.rem(c, held)

                @pl.when(hop == 0)
                def _():
                    s["run"][way, c] = s["sums"][at, way].astype(BF16)
                    rs_copy(way, c, onward).start()

                @pl.when((hop > 0) & (hop < last))
                def _():
                    rs_copy(way, c, onward).wait_recv()
                    s["run"][way, c] = (
                        s["sums"][at, way] + s["run"][way, c].astype(F32)).astype(BF16)
                    rs_copy(way, c, onward).start()

                @pl.when(hop == last)
                def _():
                    rs_copy(way, c, back).wait_recv()
                    gate = s["sums"][at, way, :, :chunk] + s["run"][way, c, :, :chunk].astype(F32)
                    up = s["sums"][at, way, :, chunk:] + s["run"][way, c, :, chunk:].astype(F32)
                    s["hid"][c, way] = (gate * jax.nn.sigmoid(gate) * up).astype(BF16)
                    ag_copy(way, c, back).start()

            g = t - SKEW * last - SKEW * (last - hop)

            @pl.when((g >= 0) & (g < chunks) & (hop < last))
            def _():
                ag_copy(way, g, onward).wait_recv()

                @pl.when(hop > 0)
                def _():
                    ag_copy(way, g, back).start()

        f = t - 2 * SKEW * last

        @pl.when((f >= 0) & (f < chunks))
        def _():
            down_load(f).wait()
            left = s["hid"][f].reshape(tokens, chunk)
            slot = lax.rem(f, DOWN_SLOTS)
            wide_tile = width_of(td.shape[1], 512)

            @pl.loop(0, td.shape[1] // wide_tile)
            def _(j):
                cols = pl.ds(pl.multiple_of(j * wide_tile, wide_tile), wide_tile)
                block = jnp.dot(left, s["d_slot"][slot, :, cols], preferred_element_type=F32)
                s["diff"][:, :, cols] = s["diff"][:, :, cols] - block.reshape(2, half, wide_tile)

            @pl.when(f + DOWN_SLOTS < chunks)
            def _():
                down_load(f + DOWN_SLOTS).start()

        for at, work in zip(wanted, plan):
            pl.when(t == at)(work)

    sum_diff.phase1()
    sum_diff.phase2()
    sum_diff.phase3()
    sum_diff.phase4()
    sum_out.drain()
    product(whole(s["ga"]), s["w_align"], s["narrow"], 0, narrow, True, False)
    sum_grad.phase1()
    sum_grad.phase2()
    sum_grad.phase3()
    sum_grad.phase4()
    sum_diff.drain()
    product(whole(s["gso"]), s["w_down"], s["diff"], 0, wide, True, False)
    sum_hidden.phase1()
    sum_hidden.phase2()

    stores = [
        pltpu.make_async_copy(s[name], out, s["o_sem"].at[i])
        for i, (name, out) in enumerate(
            [("so", o_so), ("ga", o_ga), ("sh", o_sh), ("gso", o_gso), ("gg", o_gg), ("gu", o_gu)])
    ]
    for store in stores[:4]:
        store.start()
    sum_hidden.phase3()
    sum_hidden.phase4()
    for store in stores[4:]:
        store.start()
    sum_gate.drain()
    sum_grad.drain()
    sum_hidden.drain()

    @pl.loop(0, chunks)
    def _(c):
        for way in range(2):
            hop = last - me if way == 0 else me
            onward = lax.rem(me + (tp - 1 if way == 0 else 1), tp)
            back = lax.rem(me + (1 if way == 0 else tp - 1), tp)

            @pl.when(hop < last)
            def _():
                rs_copy(way, c, onward).wait_send()

            @pl.when(hop > 0)
            def _():
                ag_copy(way, c, back).wait_send()

    for store in stores:
        store.wait()


def exchanged(x_teacher, x_student, t_gate, t_up, t_down, s_gate, s_up, s_down, align):
    tp, role = lax.axis_size("tp"), lax.axis_size("role")
    tokens, depth = x_teacher.shape
    half = tokens // 2
    units = t_gate.shape[1]
    chunk = width_of(units, 256)
    chunks = units // chunk
    wide, narrow, features = s_gate.shape[1], s_down.shape[1], align.shape[1]
    DMA = pltpu.SemaphoreType.DMA
    scratch = dict(
        sums=pltpu.VMEM((min(chunks, SKEW * (tp - 1) + 1), 2, half, 2 * chunk), F32),
        run=pltpu.VMEM((2, chunks, half, 2 * chunk), BF16),
        run_s=DMA((2, chunks)), run_r=DMA((2, chunks)),
        hid=pltpu.VMEM((chunks, 2, half, chunk), BF16),
        hid_s=DMA((2, chunks)), hid_r=DMA((2, chunks)),
        t_slot=pltpu.VMEM((TEACHER_SLOTS, 2, depth, chunk), BF16),
        t_sem=DMA((TEACHER_SLOTS, 2)),
        d_slot=pltpu.VMEM((DOWN_SLOTS, chunk, features), BF16),
        d_sem=DMA((DOWN_SLOTS,)),
        w_gate=pltpu.VMEM(s_gate.shape, BF16),
        w_down=pltpu.VMEM(s_down.shape, BF16),
        w_align=pltpu.VMEM(align.shape, BF16),
        w_sem=DMA((4,)),
        gate_up=pltpu.VMEM((2, half, 2 * wide), F32),
        narrow=pltpu.VMEM((2, half, narrow), F32),
        diff=pltpu.VMEM((2, half, max(features, wide)), F32),
        so=pltpu.VMEM((2, half, narrow), BF16),
        ga=pltpu.VMEM((2, half, features), BF16),
        sh=pltpu.VMEM((2, half, wide), BF16),
        gso=pltpu.VMEM((2, half, narrow), BF16),
        gg=pltpu.VMEM((2, half, wide), BF16),
        gu=pltpu.VMEM((2, half, wide), BF16),
        o_sem=DMA((6,)),
        b_gate=sum_scratch(role, half, 2 * wide, BF16, 1),
        b_out=sum_scratch(tp, half, narrow, BF16, 1),
        b_diff=sum_scratch(role, half, features, BF16, 1),
        b_grad=sum_scratch(tp, half, narrow, BF16, 1),
        b_hidden=sum_scratch(role, half, wide, BF16, 2),
    )
    leaves, names = jax.tree.flatten(scratch, is_leaf=lambda leaf: not isinstance(leaf, dict))
    shapes = [narrow, features, wide, narrow, wide, wide]
    outs = pl.pallas_call(
        functools.partial(exchange_kernel, names, chunk),
        out_shape=[jax.ShapeDtypeStruct((2, half, n), BF16) for n in shapes],
        in_specs=[pl.BlockSpec(memory_space=pltpu.VMEM)] * 2 + [pl.BlockSpec(memory_space=pl.ANY)] * 7,
        out_specs=[pl.BlockSpec(memory_space=pl.ANY)] * 6,
        scratch_shapes=leaves,
        compiler_params=pltpu.CompilerParams(
            collective_id=0, has_side_effects=True, vmem_limit_bytes=60 * 2**20),
        cost_estimate=pl.CostEstimate(flops=20 * 10**9, bytes_accessed=70 * 10**6, transcendentals=10**6),
    )(x_teacher, x_student, t_gate, t_up, t_down, s_gate, s_up, s_down, align)
    return [out.reshape(tokens, out.shape[2]) for out in outs]


def outer_kernel(*refs):
    count = len(refs) // 3
    for i in range(count):
        refs[2 * count + i][...] = lax.dot_general(
            refs[i][...], refs[count + i][...], (((0,), (0,)), ((), ())),
            preferred_element_type=F32).astype(BF16)


def outer_products(lefts, rights):
    tokens = lefts[0].shape[0]
    steps = min(8, min(left.shape[1] for left in lefts) // 128)
    in_specs = [pl.BlockSpec((tokens, left.shape[1] // steps), lambda i: (0, i)) for left in lefts]
    in_specs += [pl.BlockSpec(right.shape, lambda i: (0, 0)) for right in rights]
    return pl.pallas_call(
        outer_kernel,
        grid=(steps,),
        out_shape=[jax.ShapeDtypeStruct((left.shape[1], right.shape[1]), BF16)
                   for left, right in zip(lefts, rights)],
        in_specs=in_specs,
        out_specs=[pl.BlockSpec((left.shape[1] // steps, right.shape[1]), lambda i: (i, 0))
                   for left, right in zip(lefts, rights)],
        compiler_params=pltpu.CompilerParams(vmem_limit_bytes=48 * 2**20),
    )(*lefts, *rights)


def on_device(x_teacher, x_student, *weights):
    student_out, grad_aligned, student_hidden, grad_student_out, grad_gate_pre, grad_up_pre = exchanged(
        x_teacher, x_student, *weights)
    return tuple(outer_products(
        [x_student, x_student, student_hidden, student_out],
        [grad_gate_pre, grad_up_pre, grad_student_out, grad_aligned]))


def solution(mesh):
    placed = (
        P("groups", "tp"),
        P("groups", "role"),
        P("tp", "role"),
        P("tp", "role"),
        P("role", "tp"),
        P("role", "tp"),
        P("role", "tp"),
        P("tp", "role"),
        P("role", "tp"),
    )
    return jax.shard_map(
        on_device,
        mesh=mesh,
        in_specs=placed,
        out_specs=(
            P(("groups", "role"), "tp"),
            P(("groups", "role"), "tp"),
            P(("groups", "tp"), "role"),
            P(("groups", "role"), "tp"),
        ),
        check_vma=False,
    )
```

time: 432 us -> 181 us (0.42)
  waiting for transfers between devices: 216 us -> 0 us
  Pallas kernels: 0 us -> 173 us
  blocking collectives: 114 us -> 0 us
  matrix products: 61.3 us -> 0 us
  between operations: 15.8 us -> 0.67 us
  other arithmetic: 8.9 us -> 0 us
  local copies, waits for them, and re-layouts: 15.7 us -> 6.98 us
    pallas_call x0 -> x2, Pallas kernels: none -> 173 us  [the longest x1 165 us: exchanged(): pl.pallas_call(functools.partial(exchange_kernel, names, chunk), out_shap...]
    reduce_scatter x1 -> x0, waiting for transfers between devices: 122 us -> none  [tp_scatter(): lax.psum_scatter(term_fn(jnp.int32(0), lax.axis_size('tp') * share_rows),...]
    psum x2 -> x0, blocking collectives: 114 us -> none  [tp_sums(): return lax.psum(values, 'tp')]
    psum x3 -> x0, waiting for transfers between devices: 93.8 us -> none  [role_sums(): return lax.psum(values, 'role')]
    dot_general x13 -> x0, matrix products: 61.3 us -> none  [the longest x4 18.5 us: contract_rows(): lax.dot_general(left, right, (((0,), (0,)), ((), ())), preferred_element_...]
    unnamed x20 -> x14, local copies, waits for them, and re-layouts: 15.7 us -> 6.98 us
    convert_element_type x2 -> x0, other arithmetic: 5.45 us -> none  [the longest x1 2.98 us: on_device(): student_hidden = (gate_active * student_up).astype(jnp.bfloat16)]
  transfers between devices with their start and end apart: 5 -> 0, of which waited for: 3 -> 0; matrix products, arithmetic and copies ran while one was open for 5% -> 0% of each run, Pallas kernels for 0% -> 0%
where the time goes in v1:
time: 181 us
  Pallas kernels  173 us (96%)
  local copies, waits for them, and re-layouts  6.98 us (4%)
    pallas_call x1, Pallas kernels, exchanged(): pl.pallas_call(functools.partial(exchange_kernel, names, chunk), out_shap...  165 us
    pallas_call x1, Pallas kernels, outer_products(): pl.pallas_call(outer_kernel, grid=(steps,), out_shape=[jax.ShapeDtypeStru...  8.19 us
    unnamed x14, local copies, waits for them, and re-layouts  6.98 us

profile of v1, /device:TPU:0, one launch (start us, length us, event | category | flops | bytes accessed | tf_op | source)
XLA Modules:
  0.0 180.7 jit_solution(11994871650379045801)
XLA Ops:
  0.6 0.0 copy-start
  0.6 164.9 %shard_map.120 = (bf16[2,128,1024]{2,1,0:T(8,128)(2,1)}, bf16[2,128,2048]{2,1,0:T(8,128)(2,1)}, bf16[2,128,2048]{2,1,0:T(8,128)(2,1)}, bf16[2,128,1024]{2,1,0:T(...) custom-call(bf16[256,2048]{1,0:T(8,128)(2,1)} %x_t.1, bf16[256,1024]{1,0:T(8,128)(2,1)} %refs_1_.1, ...), custom_call_target="tpu_custom_call" | custom-call | flops 20000000000 | bytes 70000000 | tf_op jit(solution)/shard_map/pallas_call | solution.py:448
  165.5 0.0 copy-done
  165.6 0.0 copy-start.1
  165.6 1.2 copy-done.1
  166.8 0.0 copy-start.2
  166.8 1.2 copy-done.2
  168.0 0.0 copy-start.3
  168.0 1.2 copy-done.3
  169.2 0.0 copy-start.4
  169.2 1.2 copy-done.4
  170.5 0.0 copy-start.5
  170.5 1.0 copy-done.5
  171.5 0.0 copy-start.6
  171.5 1.0 copy-done.6
  172.5 8.2 %shard_map.121 = (bf16[1024,2048]{1,0:T(8,128)(2,1)}, bf16[1024,2048]{1,0:T(8,128)(2,1)}, bf16[2048,1024]{1,0:T(8,128)(2,1)}, bf16[1024,2048]{1,0:T(8,128)(2,1)}) custom-call(bf16[256,1024]{1,0:T(8,128)(2,1)S(1)} %copy-done, bf16[256,1024]{1,0:T(8,128)(2,1)S(1)} %copy-done, bf16[256,2048]{1,0:T(8,128)(2,1)S(1)} %bitcast.7, bf16[256,1024]{1,0:T(8,128)(2,1)S(1)} %bitcast.10, ...), custom_call_target="tpu_custom_call" | custom-call | tf_op jit(solution)/shard_map/pallas_call | solution.py:474
Async XLA Ops:
  0.6 164.9 %copy-start = (bf16[256,1024]{1,0:T(8,128)(2,1)S(1)}, bf16[256,1024]{1,0:T(8,128)(2,1)}, u32[]{:S(2)}) copy-start(bf16[256,1024]{1,0:T(8,128)(2,1)} %refs_1_.1) | copy-start | bytes 1572868
  165.6 1.2 copy-start.1
  166.8 1.2 copy-start.2
  168.0 1.2 copy-start.3
  169.2 1.2 copy-start.4
  170.5 1.0 copy-start.5
  171.5 1.0 copy-start.6

commit v2 on v1

--- a/solution.py
+++ b/solution.py
@@ -11,7 +11,8 @@
 MESH = pl.DeviceIdType.MESH
 BF16 = jnp.bfloat16
 F32 = jnp.float32
-SKEW = 2
+SKEW = 3
+GROUPS = 2
 TEACHER_SLOTS = 3
 DOWN_SLOTS = 3
 PIECES = 4
@@ -82,16 +83,16 @@
             send_sem=self.b["s3"].at[i, k], recv_sem=self.b["r3"].at[i, k],
             device_id={self.axis: self.pair}, device_id_type=MESH)
 
-    def phase1(self):
-        for k in range(PIECES):
+    def phase1(self, pieces=range(PIECES)):
+        for k in pieces:
             rows = self.rows(k)
             for cols in self.tiles():
                 self.b["sent1"][rows, cols] = self.part[1 - self.own, rows, cols].astype(
                     self.b["sent1"].dtype)
             self.copy1(k).start()
 
-    def phase2(self):
-        for k in range(PIECES):
+    def phase2(self, pieces=range(PIECES)):
+        for k in pieces:
             rows = self.rows(k)
             self.copy1(k).wait_recv()
             for cols in self.tiles():
@@ -101,8 +102,8 @@
             for j in range(self.count // 2 - 1):
                 self.copy2(j, k).start()
 
-    def phase3(self):
-        for k in range(PIECES):
+    def phase3(self, pieces=range(PIECES)):
+        for k in pieces:
             rows = self.rows(k)
             for j in range(self.count // 2 - 1):
                 self.copy2(j, k).wait_recv()
@@ -115,8 +116,8 @@
             for i in range(len(self.finals)):
                 self.copy3(i, k, self.own).start()
 
-    def phase4(self):
-        for k in range(PIECES):
+    def phase4(self, pieces=range(PIECES)):
+        for k in pieces:
             for i in range(len(self.finals)):
                 self.copy3(i, k, 1 - self.own).wait_recv()
 
@@ -129,8 +130,9 @@
                 self.copy3(i, k, self.own).wait_send()
 
 
-def whole(ref):
-    return ref[...].reshape(ref.shape[0] * ref.shape[1], ref.shape[2])
+def taken(ref, rows):
+    block = ref[:, rows]
+    return block.reshape(block.shape[0] * block.shape[1], block.shape[2])
 
 
 def exchange_kernel(names, chunk, x_t, x_s, tg, tu, td, sg, su, sd, al,
@@ -143,8 +145,13 @@
     units = tg.shape[1]
     chunks = units // chunk
     student_units = sg.shape[1]
-    held = s["sums"].shape[0]
     last = tp - 1
+    share = half // GROUPS
+    items = GROUPS * chunks
+    every = pl.ds(0, half)
+    of_group = [pl.ds(g * share, share) for g in range(GROUPS)]
+    per_group = PIECES // GROUPS
+    pieces = [range(g * per_group, (g + 1) * per_group) for g in range(GROUPS)]
 
     def teacher_load(c):
         cols = pl.ds(pl.multiple_of(c * chunk, chunk), chunk)
@@ -154,11 +161,11 @@
             pltpu.make_async_copy(tu.at[:, cols], s["t_slot"].at[slot, 1], s["t_sem"].at[slot, 1]),
         )
 
-    def down_load(c):
-        slot = lax.rem(c, DOWN_SLOTS)
+    def down_load(i):
+        slot = lax.rem(i, DOWN_SLOTS)
+        first = pl.multiple_of(lax.rem(i, chunks) * chunk, chunk)
         return pltpu.make_async_copy(
-            td.at[pl.ds(pl.multiple_of(c * chunk, chunk), chunk)],
-            s["d_slot"].at[slot], s["d_sem"].at[slot])
+            td.at[pl.ds(first, chunk)], s["d_slot"].at[slot], s["d_sem"].at[slot])
 
     load_sg = pltpu.make_async_copy(sg, s["w_gate"], s["w_sem"].at[0])
     load_su = pltpu.make_async_copy(su, s["w_gate"], s["w_sem"].at[1])
@@ -171,7 +178,7 @@
     load_sg.start()
     load_sd.start()
     load_al.start()
-    for c in range(min(DOWN_SLOTS, chunks)):
+    for c in range(min(DOWN_SLOTS, items)):
         down_load(c).start()
 
     barrier = pltpu.get_barrier_semaphore()
@@ -232,7 +239,7 @@
     sum_hidden = Summed("role", s["diff"], wide, s["b_hidden"], [s["gg"], s["gu"]],
                         finish_grad_hidden)
 
-    def product(left, right, out, first_col, columns, transposed, add):
+    def product(left, right, out, rows, first_col, columns, transposed, add):
         tile = width_of(columns, 256)
 
         @pl.loop(0, columns // tile)
@@ -243,38 +250,58 @@
                                         preferred_element_type=F32)
             else:
                 block = jnp.dot(left, right[:, pl.ds(at, tile)], preferred_element_type=F32)
-            block = block.reshape(2, half, tile)
+            block = block.reshape(2, block.shape[0] // 2, tile)
             cols = pl.ds(pl.multiple_of(first_col + at, tile), tile)
             if add:
-                out[:, :, cols] = out[:, :, cols] + block
+                out[:, rows, cols] = out[:, rows, cols] + block
             else:
-                out[:, :, cols] = block
+                out[:, rows, cols] = block
 
     def student_gate():
         load_sg.wait()
-        product(x_s[...], s["w_gate"], s["gate_up"], 0, student_units, False, False)
+        product(x_s[...], s["w_gate"], s["gate_up"], every, 0, student_units, False, False)
         load_su.start()
 
     def student_up():
         load_su.wait()
-        product(x_s[...], s["w_gate"], s["gate_up"], student_units, student_units, False, False)
+        product(x_s[...], s["w_gate"], s["gate_up"], every, student_units, student_units, False, False)
         sum_gate.phase1()
 
     def student_down():
         sum_gate.phase4()
         load_sd.wait()
-        product(whole(s["sh"]), s["w_down"], s["narrow"], 0, narrow, False, False)
+        product(taken(s["sh"], every), s["w_down"], s["narrow"], every, 0, narrow, False, False)
         sum_out.phase1()
 
     def student_align():
         sum_out.phase4()
         load_al.wait()
-        product(whole(s["so"]), s["w_align"], s["diff"], 0, al.shape[1], False, True)
-
-    steps = max(chunks + 2 * SKEW * last, 18)
-    plan = [student_gate, student_up, sum_gate.phase2, sum_gate.phase3, student_down,
-            sum_out.phase2, sum_out.phase3, student_align]
-    wanted = [1, 2, 3, 9, 10, 12, 15, 17]
+        product(taken(s["so"], every), s["w_align"], s["diff"], every, 0, al.shape[1], False, True)
+
+    def grad_out(g):
+        sum_diff.phase4(pieces[g])
+        product(taken(s["ga"], of_group[g]), s["w_align"], s["narrow"], of_group[g], 0, narrow,
+                True, False)
+        sum_grad.phase1(pieces[g])
+
+    def grad_hidden(g):
+        sum_grad.phase4(pieces[g])
+        product(taken(s["gso"], of_group[g]), s["w_down"], s["diff"], of_group[g], 0, wide,
+                True, False)
+        sum_hidden.phase1(pieces[g])
+
+    first_done = chunks - 1 + 2 * SKEW * last
+    plan = {
+        1: student_gate, 2: student_up, 4: sum_gate.phase2, 16: sum_gate.phase3,
+        18: student_down, 21: sum_out.phase2, 26: sum_out.phase3, 29: student_align,
+        first_done: lambda: sum_diff.phase1(pieces[0]),
+        first_done + 1: lambda: sum_diff.phase2(pieces[0]),
+        first_done + 5: lambda: sum_diff.phase3(pieces[0]),
+        first_done + 6: lambda: grad_out(0),
+        first_done + 8: lambda: sum_grad.phase2(pieces[0]),
+        first_done + 12: lambda: sum_grad.phase3(pieces[0]),
+    }
+    steps = max(items + 2 * SKEW * last, first_done + 13)
 
     @pl.loop(0, steps)
     def _(t):
@@ -285,7 +312,7 @@
             slot = lax.rem(t, TEACHER_SLOTS)
             for k in range(2):
                 block = jnp.dot(x_t[...], s["t_slot"][slot, k], preferred_element_type=F32)
-                s["sums"][lax.rem(t, held), :, :, k * chunk:(k + 1) * chunk] = block.reshape(
+                s["sums"][t, :, :, k * chunk:(k + 1) * chunk] = block.reshape(
                     2, half, chunk)
 
             @pl.when(t + TEACHER_SLOTS < chunks)
@@ -299,33 +326,34 @@
             back = lax.rem(me + (1 if way == 0 else tp - 1), tp)
             c = t - SKEW * hop
 
-            @pl.when((c >= 0) & (c < chunks))
+            @pl.when((c >= 0) & (c < items))
             def _():
-                at = lax.rem(c, held)
+                at = lax.rem(c, chunks)
+                mine = pl.ds(pl.multiple_of(lax.div(c, chunks) * share, share), share)
 
                 @pl.when(hop == 0)
                 def _():
-                    s["run"][way, c] = s["sums"][at, way].astype(BF16)
+                    s["run"][way, c] = s["sums"][at, way, mine].astype(BF16)
                     rs_copy(way, c, onward).start()
 
                 @pl.when((hop > 0) & (hop < last))
                 def _():
                     rs_copy(way, c, onward).wait_recv()
                     s["run"][way, c] = (
-                        s["sums"][at, way] + s["run"][way, c].astype(F32)).astype(BF16)
+                        s["sums"][at, way, mine] + s["run"][way, c].astype(F32)).astype(BF16)
                     rs_copy(way, c, onward).start()
 
                 @pl.when(hop == last)
                 def _():
                     rs_copy(way, c, back).wait_recv()
-                    gate = s["sums"][at, way, :, :chunk] + s["run"][way, c, :, :chunk].astype(F32)
-                    up = s["sums"][at, way, :, chunk:] + s["run"][way, c, :, chunk:].astype(F32)
+                    gate = s["sums"][at, way, mine, :chunk] + s["run"][way, c, :, :chunk].astype(F32)
+                    up = s["sums"][at, way, mine, chunk:] + s["run"][way, c, :, chunk:].astype(F32)
                     s["hid"][c, way] = (gate * jax.nn.sigmoid(gate) * up).astype(BF16)
                     ag_copy(way, c, back).start()
 
             g = t - SKEW * last - SKEW * (last - hop)
 
-            @pl.when((g >= 0) & (g < chunks) & (hop < last))
+            @pl.when((g >= 0) & (g < items) & (hop < last))
             def _():
                 ag_copy(way, g, onward).wait_recv()
 
@@ -335,10 +363,11 @@
 
         f = t - 2 * SKEW * last
 
-        @pl.when((f >= 0) & (f < chunks))
+        @pl.when((f >= 0) & (f < items))
         def _():
             down_load(f).wait()
-            left = s["hid"][f].reshape(tokens, chunk)
+            left = s["hid"][f].reshape(2 * share, chunk)
+            mine = pl.ds(pl.multiple_of(lax.div(f, chunks) * share, share), share)
             slot = lax.rem(f, DOWN_SLOTS)
             wide_tile = width_of(td.shape[1], 512)
 
@@ -346,29 +375,26 @@
             def _(j):
                 cols = pl.ds(pl.multiple_of(j * wide_tile, wide_tile), wide_tile)
                 block = jnp.dot(left, s["d_slot"][slot, :, cols], preferred_element_type=F32)
-                s["diff"][:, :, cols] = s["diff"][:, :, cols] - block.reshape(2, half, wide_tile)
-
-            @pl.when(f + DOWN_SLOTS < chunks)
+                s["diff"][:, mine, cols] = s["diff"][:, mine, cols] - block.reshape(2, share, wide_tile)
+
+            @pl.when(f + DOWN_SLOTS < items)
             def _():
                 down_load(f + DOWN_SLOTS).start()
 
-        for at, work in zip(wanted, plan):
+        for at, work in plan.items():
             pl.when(t == at)(work)
 
-    sum_diff.phase1()
-    sum_diff.phase2()
-    sum_diff.phase3()
-    sum_diff.phase4()
-    sum_out.drain()
-    product(whole(s["ga"]), s["w_align"], s["narrow"], 0, narrow, True, False)
-    sum_grad.phase1()
-    sum_grad.phase2()
-    sum_grad.phase3()
-    sum_grad.phase4()
-    sum_diff.drain()
-    product(whole(s["gso"]), s["w_down"], s["diff"], 0, wide, True, False)
-    sum_hidden.phase1()
-    sum_hidden.phase2()
+    sum_diff.phase1(pieces[1])
+    sum_diff.phase2(pieces[1])
+    grad_hidden(0)
+    sum_hidden.phase2(pieces[0])
+    sum_diff.phase3(pieces[1])
+    grad_out(1)
+    sum_grad.phase2(pieces[1])
+    sum_hidden.phase3(pieces[0])
+    sum_grad.phase3(pieces[1])
+    grad_hidden(1)
+    sum_hidden.phase2(pieces[1])
 
     stores = [
         pltpu.make_async_copy(s[name], out, s["o_sem"].at[i])
@@ -377,15 +403,17 @@
     ]
     for store in stores[:4]:
         store.start()
-    sum_hidden.phase3()
+    sum_hidden.phase3(pieces[1])
     sum_hidden.phase4()
     for store in stores[4:]:
         store.start()
     sum_gate.drain()
+    sum_out.drain()
+    sum_diff.drain()
     sum_grad.drain()
     sum_hidden.drain()
 
-    @pl.loop(0, chunks)
+    @pl.loop(0, items)
     def _(c):
         for way in range(2):
             hop = last - me if way == 0 else me
@@ -411,14 +439,16 @@
     units = t_gate.shape[1]
     chunk = width_of(units, 256)
     chunks = units // chunk
+    items = GROUPS * chunks
+    share = half // GROUPS
     wide, narrow, features = s_gate.shape[1], s_down.shape[1], align.shape[1]
     DMA = pltpu.SemaphoreType.DMA
     scratch = dict(
-        sums=pltpu.VMEM((min(chunks, SKEW * (tp - 1) + 1), 2, half, 2 * chunk), F32),
-        run=pltpu.VMEM((2, chunks, half, 2 * chunk), BF16),
-        run_s=DMA((2, chunks)), run_r=DMA((2, chunks)),
-        hid=pltpu.VMEM((chunks, 2, half, chunk), BF16),
-        hid_s=DMA((2, chunks)), hid_r=DMA((2, chunks)),
+        sums=pltpu.VMEM((chunks, 2, half, 2 * chunk), F32),
+        run=pltpu.VMEM((2, items, share, 2 * chunk), BF16),
+        run_s=DMA((2, items)), run_r=DMA((2, items)),
+        hid=pltpu.VMEM((items, 2, share, chunk), BF16),
+        hid_s=DMA((2, items)), hid_r=DMA((2, items)),
         t_slot=pltpu.VMEM((TEACHER_SLOTS, 2, depth, chunk), BF16),
         t_sem=DMA((TEACHER_SLOTS, 2)),
         d_slot=pltpu.VMEM((DOWN_SLOTS, chunk, features), BF16),
@@ -479,7 +509,7 @@
         in_specs=in_specs,
         out_specs=[pl.BlockSpec((left.shape[1] // steps, right.shape[1]), lambda i: (i, 0))
                    for left, right in zip(lefts, rights)],
-        compiler_params=pltpu.CompilerParams(vmem_limit_bytes=48 * 2**20),
+        compiler_params=pltpu.CompilerParams(vmem_limit_bytes=60 * 2**20),
     )(*lefts, *rights)
 
 

time: 181 us -> 169 us (0.934)
  local copies, waits for them, and re-layouts: 6.98 us -> 0 us
  Pallas kernels: 173 us -> 167 us
    pallas_call x1, Pallas kernels: 165 us -> 156 us  [exchanged(): pl.pallas_call(functools.partial(exchange_kernel, names, chunk), out_shap...]
    unnamed x14 -> x0, local copies, waits for them, and re-layouts: 6.98 us -> none
    pallas_call x1, Pallas kernels: 8.19 us -> 11.2 us  [outer_products(): pl.pallas_call(outer_kernel, grid=(steps,), out_shape=[jax.ShapeDtypeStru...]
where the time goes in v2:
time: 169 us; the launch traced here: 167 us
  Pallas kernels  167 us (99%)
    pallas_call x1, Pallas kernels, exchanged(): pl.pallas_call(functools.partial(exchange_kernel, names, chunk), out_shap...  156 us
    pallas_call x1, Pallas kernels, outer_products(): pl.pallas_call(outer_kernel, grid=(steps,), out_shape=[jax.ShapeDtypeStru...  11.2 us

profile of v2, /device:TPU:0, one launch (start us, length us, event | category | flops | bytes accessed | tf_op | source)
XLA Modules:
  0.0 167.5 jit_solution(3916079282500459311)
XLA Ops:
  0.6 155.7 %shard_map.120 = (bf16[2,128,1024]{2,1,0:T(8,128)(2,1)}, bf16[2,128,2048]{2,1,0:T(8,128)(2,1)}, bf16[2,128,2048]{2,1,0:T(8,128)(2,1)}, bf16[2,128,1024]{2,1,0:T(...) custom-call(bf16[256,2048]{1,0:T(8,128)(2,1)} %x_t.1, bf16[256,1024]{1,0:T(8,128)(2,1)} %refs_1_.1, ...), custom_call_target="tpu_custom_call" | custom-call | flops 20000000000 | bytes 70000000 | tf_op jit(solution)/shard_map/pallas_call | solution.py:478
  156.3 11.2 %shard_map.121 = (bf16[1024,2048]{1,0:T(8,128)(2,1)}, bf16[1024,2048]{1,0:T(8,128)(2,1)}, bf16[2048,1024]{1,0:T(8,128)(2,1)}, bf16[1024,2048]{1,0:T(8,128)(2,1)}) custom-call(bf16[256,1024]{1,0:T(8,128)(2,1)} %refs_1_.1, bf16[256,1024]{1,0:T(8,128)(2,1)} %refs_1_.1, bf16[256,2048]{1,0:T(8,128)(2,1)} %bitcast.7, bf16[256,1024]{1,0:T(8,128)(2,1)} %bitcast.10, ...), custom_call_target="tpu_custom_call" | custom-call | tf_op jit(solution)/shard_map/pallas_call | solution.py:504

commit v3 on v2

--- a/solution.py
+++ b/solution.py
@@ -267,16 +267,20 @@
         product(x_s[...], s["w_gate"], s["gate_up"], every, student_units, student_units, False, False)
         sum_gate.phase1()
 
-    def student_down():
-        sum_gate.phase4()
-        load_sd.wait()
-        product(taken(s["sh"], every), s["w_down"], s["narrow"], every, 0, narrow, False, False)
-        sum_out.phase1()
-
-    def student_align():
-        sum_out.phase4()
-        load_al.wait()
-        product(taken(s["so"], every), s["w_align"], s["diff"], every, 0, al.shape[1], False, True)
+    def student_down(g):
+        sum_gate.phase4(pieces[g])
+        if g == 0:
+            load_sd.wait()
+        product(taken(s["sh"], of_group[g]), s["w_down"], s["narrow"], of_group[g], 0, narrow,
+                False, False)
+        sum_out.phase1(pieces[g])
+
+    def student_align(g):
+        sum_out.phase4(pieces[g])
+        if g == 0:
+            load_al.wait()
+        product(taken(s["so"], of_group[g]), s["w_align"], s["diff"], of_group[g], 0, al.shape[1],
+                False, True)
 
     def grad_out(g):
         sum_diff.phase4(pieces[g])
@@ -290,18 +294,28 @@
                 True, False)
         sum_hidden.phase1(pieces[g])
 
-    first_done = chunks - 1 + 2 * SKEW * last
-    plan = {
-        1: student_gate, 2: student_up, 4: sum_gate.phase2, 16: sum_gate.phase3,
-        18: student_down, 21: sum_out.phase2, 26: sum_out.phase3, 29: student_align,
-        first_done: lambda: sum_diff.phase1(pieces[0]),
-        first_done + 1: lambda: sum_diff.phase2(pieces[0]),
-        first_done + 5: lambda: sum_diff.phase3(pieces[0]),
-        first_done + 6: lambda: grad_out(0),
-        first_done + 8: lambda: sum_grad.phase2(pieces[0]),
-        first_done + 12: lambda: sum_grad.phase3(pieces[0]),
-    }
-    steps = max(items + 2 * SKEW * last, first_done + 13)
+    first_done = max(chunks - 1 + 2 * SKEW * last, 28)
+    plan = [
+        (1, student_gate),
+        (2, student_up),
+        (4, sum_gate.phase2),
+        (11, lambda: sum_gate.phase3(pieces[0])),
+        (12, lambda: student_down(0)),
+        (16, lambda: sum_out.phase2(pieces[0])),
+        (18, lambda: sum_gate.phase3(pieces[1])),
+        (19, lambda: student_down(1)),
+        (22, lambda: sum_out.phase3(pieces[0])),
+        (24, lambda: sum_out.phase2(pieces[1])),
+        (26, lambda: student_align(0)),
+        (30, lambda: sum_out.phase3(pieces[1])),
+        (first_done, lambda: sum_diff.phase1(pieces[0])),
+        (first_done + 1, lambda: sum_diff.phase2(pieces[0])),
+        (34, lambda: student_align(1)),
+        (first_done + 6, lambda: sum_diff.phase3(pieces[0])),
+        (first_done + 7, lambda: grad_out(0)),
+        (first_done + 11, lambda: sum_grad.phase2(pieces[0])),
+    ]
+    steps = max(items + 2 * SKEW * last, first_done + 12)
 
     @pl.loop(0, steps)
     def _(t):
@@ -381,17 +395,18 @@
             def _():
                 down_load(f + DOWN_SLOTS).start()
 
-        for at, work in plan.items():
+        for at, work in plan:
             pl.when(t == at)(work)
 
     sum_diff.phase1(pieces[1])
+    sum_grad.phase3(pieces[0])
     sum_diff.phase2(pieces[1])
     grad_hidden(0)
     sum_hidden.phase2(pieces[0])
     sum_diff.phase3(pieces[1])
     grad_out(1)
+    sum_hidden.phase3(pieces[0])
     sum_grad.phase2(pieces[1])
-    sum_hidden.phase3(pieces[0])
     sum_grad.phase3(pieces[1])
     grad_hidden(1)
     sum_hidden.phase2(pieces[1])
@@ -498,7 +513,7 @@
 
 def outer_products(lefts, rights):
     tokens = lefts[0].shape[0]
-    steps = min(8, min(left.shape[1] for left in lefts) // 128)
+    steps = min(4, min(left.shape[1] for left in lefts) // 128)
     in_specs = [pl.BlockSpec((tokens, left.shape[1] // steps), lambda i: (0, i)) for left in lefts]
     in_specs += [pl.BlockSpec(right.shape, lambda i: (0, 0)) for right in rights]
     return pl.pallas_call(

time: 169 us -> 165 us (0.976)
  Pallas kernels: 167 us -> 164 us
    pallas_call x1, Pallas kernels: 11.2 us -> 9.39 us  [outer_products(): pl.pallas_call(outer_kernel, grid=(steps,), out_shape=[jax.ShapeDtypeStru...]
where the time goes in v3:
time: 165 us
  Pallas kernels  164 us (99%)
    pallas_call x1, Pallas kernels, exchanged(): pl.pallas_call(functools.partial(exchange_kernel, names, chunk), out_shap...  155 us
    pallas_call x1, Pallas kernels, outer_products(): pl.pallas_call(outer_kernel, grid=(steps,), out_shape=[jax.ShapeDtypeStru...  9.39 us

profile of v3, /device:TPU:0, one launch (start us, length us, event | category | flops | bytes accessed | tf_op | source)
XLA Modules:
  0.0 164.9 jit_solution(4730748758270983211)
XLA Ops:
  0.6 154.9 %shard_map.120 = (bf16[2,128,1024]{2,1,0:T(8,128)(2,1)}, bf16[2,128,2048]{2,1,0:T(8,128)(2,1)}, bf16[2,128,2048]{2,1,0:T(8,128)(2,1)}, bf16[2,128,1024]{2,1,0:T(...) custom-call(bf16[256,2048]{1,0:T(8,128)(2,1)} %x_t.1, bf16[256,1024]{1,0:T(8,128)(2,1)} %refs_1_.1, ...), custom_call_target="tpu_custom_call" | custom-call | flops 20000000000 | bytes 70000000 | tf_op jit(solution)/shard_map/pallas_call | solution.py:493
  155.5 9.4 %shard_map.121 = (bf16[1024,2048]{1,0:T(8,128)(2,1)}, bf16[1024,2048]{1,0:T(8,128)(2,1)}, bf16[2048,1024]{1,0:T(8,128)(2,1)}, bf16[1024,2048]{1,0:T(8,128)(2,1)}) custom-call(bf16[256,1024]{1,0:T(8,128)(2,1)} %refs_1_.1, bf16[256,1024]{1,0:T(8,128)(2,1)} %refs_1_.1, bf16[256,2048]{1,0:T(8,128)(2,1)} %bitcast.7, bf16[256,1024]{1,0:T(8,128)(2,1)} %bitcast.10, ...), custom_call_target="tpu_custom_call" | custom-call | tf_op jit(solution)/shard_map/pallas_call | solution.py:519

commit v4 on v3

--- a/solution.py
+++ b/solution.py
@@ -157,8 +157,8 @@
         cols = pl.ds(pl.multiple_of(c * chunk, chunk), chunk)
         slot = lax.rem(c, TEACHER_SLOTS)
         return (
-            pltpu.make_async_copy(tg.at[:, cols], s["t_slot"].at[slot, 0], s["t_sem"].at[slot, 0]),
-            pltpu.make_async_copy(tu.at[:, cols], s["t_slot"].at[slot, 1], s["t_sem"].at[slot, 1]),
+            pltpu.make_async_copy(tg.at[:, cols], s["t_slot"].at[slot, :, :chunk], s["t_sem"].at[slot, 0]),
+            pltpu.make_async_copy(tu.at[:, cols], s["t_slot"].at[slot, :, chunk:], s["t_sem"].at[slot, 1]),
         )
 
     def down_load(i):
@@ -240,7 +240,7 @@
                         finish_grad_hidden)
 
     def product(left, right, out, rows, first_col, columns, transposed, add):
-        tile = width_of(columns, 256)
+        tile = width_of(columns, 512 if transposed else 1024)
 
         @pl.loop(0, columns // tile)
         def _(j):
@@ -282,17 +282,21 @@
         product(taken(s["so"], of_group[g]), s["w_align"], s["diff"], of_group[g], 0, al.shape[1],
                 False, True)
 
-    def grad_out(g):
-        sum_diff.phase4(pieces[g])
-        product(taken(s["ga"], of_group[g]), s["w_align"], s["narrow"], of_group[g], 0, narrow,
-                True, False)
-        sum_grad.phase1(pieces[g])
-
-    def grad_hidden(g):
-        sum_grad.phase4(pieces[g])
-        product(taken(s["gso"], of_group[g]), s["w_down"], s["diff"], of_group[g], 0, wide,
-                True, False)
-        sum_hidden.phase1(pieces[g])
+    def rows_of(some):
+        step = half // PIECES
+        return pl.ds(some[0] * step, len(some) * step)
+
+    def grad_out(some):
+        rows = rows_of(some)
+        sum_diff.phase4(some)
+        product(taken(s["ga"], rows), s["w_align"], s["narrow"], rows, 0, narrow, True, False)
+        sum_grad.phase1(some)
+
+    def grad_hidden(some):
+        rows = rows_of(some)
+        sum_grad.phase4(some)
+        product(taken(s["gso"], rows), s["w_down"], s["diff"], rows, 0, wide, True, False)
+        sum_hidden.phase1(some)
 
     first_done = max(chunks - 1 + 2 * SKEW * last, 28)
     plan = [
@@ -311,11 +315,12 @@
         (first_done, lambda: sum_diff.phase1(pieces[0])),
         (first_done + 1, lambda: sum_diff.phase2(pieces[0])),
         (34, lambda: student_align(1)),
-        (first_done + 6, lambda: sum_diff.phase3(pieces[0])),
-        (first_done + 7, lambda: grad_out(0)),
-        (first_done + 11, lambda: sum_grad.phase2(pieces[0])),
+        (first_done + 5, lambda: sum_diff.phase3(pieces[0])),
+        (first_done + 6, lambda: grad_out(pieces[0])),
+        (first_done + 9, lambda: sum_grad.phase2(pieces[0])),
+        (first_done + 13, lambda: sum_grad.phase3(pieces[0])),
     ]
-    steps = max(items + 2 * SKEW * last, first_done + 12)
+    steps = max(items + 2 * SKEW * last, first_done + 14)
 
     @pl.loop(0, steps)
     def _(t):
@@ -324,10 +329,8 @@
             for load in teacher_load(t):
                 load.wait()
             slot = lax.rem(t, TEACHER_SLOTS)
-            for k in range(2):
-                block = jnp.dot(x_t[...], s["t_slot"][slot, k], preferred_element_type=F32)
-                s["sums"][t, :, :, k * chunk:(k + 1) * chunk] = block.reshape(
-                    2, half, chunk)
+            block = jnp.dot(x_t[...], s["t_slot"][slot], preferred_element_type=F32)
+            s["sums"][t] = block.reshape(2, half, 2 * chunk)
 
             @pl.when(t + TEACHER_SLOTS < chunks)
             def _():
@@ -383,7 +386,7 @@
             left = s["hid"][f].reshape(2 * share, chunk)
             mine = pl.ds(pl.multiple_of(lax.div(f, chunks) * share, share), share)
             slot = lax.rem(f, DOWN_SLOTS)
-            wide_tile = width_of(td.shape[1], 512)
+            wide_tile = width_of(td.shape[1], 2048)
 
             @pl.loop(0, td.shape[1] // wide_tile)
             def _(j):
@@ -398,18 +401,24 @@
         for at, work in plan:
             pl.when(t == at)(work)
 
+    single = [[k] for k in pieces[1]]
     sum_diff.phase1(pieces[1])
-    sum_grad.phase3(pieces[0])
     sum_diff.phase2(pieces[1])
-    grad_hidden(0)
+    grad_hidden(pieces[0])
     sum_hidden.phase2(pieces[0])
-    sum_diff.phase3(pieces[1])
-    grad_out(1)
+    for k in single:
+        sum_diff.phase3(k)
+    for k in single:
+        grad_out(k)
     sum_hidden.phase3(pieces[0])
-    sum_grad.phase2(pieces[1])
-    sum_grad.phase3(pieces[1])
-    grad_hidden(1)
-    sum_hidden.phase2(pieces[1])
+    for k in single:
+        sum_grad.phase2(k)
+    for k in single:
+        sum_grad.phase3(k)
+    for k in single:
+        grad_hidden(k)
+    for k in single:
+        sum_hidden.phase2(k)
 
     stores = [
         pltpu.make_async_copy(s[name], out, s["o_sem"].at[i])
@@ -464,7 +473,7 @@
         run_s=DMA((2, items)), run_r=DMA((2, items)),
         hid=pltpu.VMEM((items, 2, share, chunk), BF16),
         hid_s=DMA((2, items)), hid_r=DMA((2, items)),
-        t_slot=pltpu.VMEM((TEACHER_SLOTS, 2, depth, chunk), BF16),
+        t_slot=pltpu.VMEM((TEACHER_SLOTS, depth, 2 * chunk), BF16),
         t_sem=DMA((TEACHER_SLOTS, 2)),
         d_slot=pltpu.VMEM((DOWN_SLOTS, chunk, features), BF16),
         d_sem=DMA((DOWN_SLOTS,)),

time: 165 us -> 161 us (0.976)
  Pallas kernels: 164 us -> 159 us
    pallas_call x1, Pallas kernels: 155 us -> 150 us  [exchanged(): pl.pallas_call(functools.partial(exchange_kernel, names, chunk), out_shap...]
where the time goes in v4:
time: 161 us; the launch traced here: 160 us
  Pallas kernels  159 us (99%)
    pallas_call x1, Pallas kernels, exchanged(): pl.pallas_call(functools.partial(exchange_kernel, names, chunk), out_shap...  150 us
    pallas_call x1, Pallas kernels, outer_products(): pl.pallas_call(outer_kernel, grid=(steps,), out_shape=[jax.ShapeDtypeStru...  9.39 us

profile of v4, /device:TPU:0, one launch (start us, length us, event | category | flops | bytes accessed | tf_op | source)
XLA Modules:
  0.0 160.1 jit_solution(5667440222160077211)
XLA Ops:
  0.6 150.1 %shard_map.120 = (bf16[2,128,1024]{2,1,0:T(8,128)(2,1)}, bf16[2,128,2048]{2,1,0:T(8,128)(2,1)}, bf16[2,128,2048]{2,1,0:T(8,128)(2,1)}, bf16[2,128,1024]{2,1,0:T(...) custom-call(bf16[256,2048]{1,0:T(8,128)(2,1)} %x_t.1, bf16[256,1024]{1,0:T(8,128)(2,1)} %refs_1_.1, ...), custom_call_target="tpu_custom_call" | custom-call | flops 20000000000 | bytes 70000000 | tf_op jit(solution)/shard_map/pallas_call | solution.py:502
  150.7 9.4 %shard_map.121 = (bf16[1024,2048]{1,0:T(8,128)(2,1)}, bf16[1024,2048]{1,0:T(8,128)(2,1)}, bf16[2048,1024]{1,0:T(8,128)(2,1)}, bf16[1024,2048]{1,0:T(8,128)(2,1)}) custom-call(bf16[256,1024]{1,0:T(8,128)(2,1)} %refs_1_.1, bf16[256,1024]{1,0:T(8,128)(2,1)} %refs_1_.1, bf16[256,2048]{1,0:T(8,128)(2,1)} %bitcast.7, bf16[256,1024]{1,0:T(8,128)(2,1)} %bitcast.10, ...), custom_call_target="tpu_custom_call" | custom-call | tf_op jit(solution)/shard_map/pallas_call | solution.py:528

commit v5 on v4

--- a/solution.py
+++ b/solution.py
@@ -12,7 +12,7 @@
 BF16 = jnp.bfloat16
 F32 = jnp.float32
 SKEW = 3
-GROUPS = 2
+GROUPS = 4
 TEACHER_SLOTS = 3
 DOWN_SLOTS = 3
 PIECES = 4
@@ -149,9 +149,10 @@
     share = half // GROUPS
     items = GROUPS * chunks
     every = pl.ds(0, half)
-    of_group = [pl.ds(g * share, share) for g in range(GROUPS)]
+    of_group = [pl.ds(g * (half // 2), half // 2) for g in range(2)]
+    pieces = [range(g * PIECES // 2, (g + 1) * PIECES // 2) for g in range(2)]
     per_group = PIECES // GROUPS
-    pieces = [range(g * per_group, (g + 1) * per_group) for g in range(GROUPS)]
+    group = [range(g * per_group, (g + 1) * per_group) for g in range(GROUPS)]
 
     def teacher_load(c):
         cols = pl.ds(pl.multiple_of(c * chunk, chunk), chunk)
@@ -298,29 +299,39 @@
         product(taken(s["gso"], rows), s["w_down"], s["diff"], rows, 0, wide, True, False)
         sum_hidden.phase1(some)
 
-    first_done = max(chunks - 1 + 2 * SKEW * last, 28)
     plan = [
         (1, student_gate),
         (2, student_up),
         (4, sum_gate.phase2),
-        (11, lambda: sum_gate.phase3(pieces[0])),
-        (12, lambda: student_down(0)),
-        (16, lambda: sum_out.phase2(pieces[0])),
-        (18, lambda: sum_gate.phase3(pieces[1])),
-        (19, lambda: student_down(1)),
-        (22, lambda: sum_out.phase3(pieces[0])),
-        (24, lambda: sum_out.phase2(pieces[1])),
-        (26, lambda: student_align(0)),
-        (30, lambda: sum_out.phase3(pieces[1])),
-        (first_done, lambda: sum_diff.phase1(pieces[0])),
-        (first_done + 1, lambda: sum_diff.phase2(pieces[0])),
-        (34, lambda: student_align(1)),
-        (first_done + 5, lambda: sum_diff.phase3(pieces[0])),
-        (first_done + 6, lambda: grad_out(pieces[0])),
-        (first_done + 9, lambda: sum_grad.phase2(pieces[0])),
-        (first_done + 13, lambda: sum_grad.phase3(pieces[0])),
+        (13, lambda: sum_gate.phase3(pieces[0])),
+        (14, lambda: student_down(0)),
+        (19, lambda: sum_out.phase2(pieces[0])),
+        (22, lambda: sum_gate.phase3(pieces[1])),
+        (23, lambda: student_down(1)),
+        (27, lambda: sum_out.phase3(pieces[0])),
+        (29, lambda: sum_out.phase2(pieces[1])),
+        (32, lambda: student_align(0)),
+        (38, lambda: sum_out.phase3(pieces[1])),
+        (39, lambda: student_align(1)),
     ]
-    steps = max(items + 2 * SKEW * last, first_done + 14)
+    for g in range(GROUPS - 1):
+        start = max((g + 1) * chunks - 1 + 2 * SKEW * last, 40)
+        some = group[g]
+        plan += [
+            (start, functools.partial(sum_diff.phase1, some)),
+            (start + 1, functools.partial(sum_diff.phase2, some)),
+            (start + 5, functools.partial(sum_diff.phase3, some)),
+            (start + 6, functools.partial(grad_out, some)),
+            (start + 9, functools.partial(sum_grad.phase2, some)),
+            (start + 13, functools.partial(sum_grad.phase3, some)),
+        ]
+        if g < GROUPS - 2:
+            plan += [
+                (start + 14, functools.partial(grad_hidden, some)),
+                (start + 15, functools.partial(sum_hidden.phase2, some)),
+                (start + 20, functools.partial(sum_hidden.phase3, some)),
+            ]
+    steps = max([items + 2 * SKEW * last] + [at + 1 for at, _ in plan])
 
     @pl.loop(0, steps)
     def _(t):
@@ -401,24 +412,18 @@
         for at, work in plan:
             pl.when(t == at)(work)
 
-    single = [[k] for k in pieces[1]]
-    sum_diff.phase1(pieces[1])
-    sum_diff.phase2(pieces[1])
-    grad_hidden(pieces[0])
-    sum_hidden.phase2(pieces[0])
-    for k in single:
-        sum_diff.phase3(k)
-    for k in single:
-        grad_out(k)
-    sum_hidden.phase3(pieces[0])
-    for k in single:
-        sum_grad.phase2(k)
-    for k in single:
-        sum_grad.phase3(k)
-    for k in single:
-        grad_hidden(k)
-    for k in single:
-        sum_hidden.phase2(k)
+    late, final = group[-2], group[-1]
+    sum_diff.phase1(final)
+    sum_diff.phase2(final)
+    grad_hidden(late)
+    sum_hidden.phase2(late)
+    sum_diff.phase3(final)
+    grad_out(final)
+    sum_hidden.phase3(late)
+    sum_grad.phase2(final)
+    sum_grad.phase3(final)
+    grad_hidden(final)
+    sum_hidden.phase2(final)
 
     stores = [
         pltpu.make_async_copy(s[name], out, s["o_sem"].at[i])
@@ -427,7 +432,7 @@
     ]
     for store in stores[:4]:
         store.start()
-    sum_hidden.phase3(pieces[1])
+    sum_hidden.phase3(final)
     sum_hidden.phase4()
     for store in stores[4:]:
         store.start()

time: 161 us -> 184 us (1.14)
  Pallas kernels: 159 us -> 183 us
    pallas_call x1, Pallas kernels: 150 us -> 174 us  [exchanged(): pl.pallas_call(functools.partial(exchange_kernel, names, chunk), out_shap...]
where the time goes in v5:
time: 184 us
  Pallas kernels  183 us (99%)
    pallas_call x1, Pallas kernels, exchanged(): pl.pallas_call(functools.partial(exchange_kernel, names, chunk), out_shap...  174 us
    pallas_call x1, Pallas kernels, outer_products(): pl.pallas_call(outer_kernel, grid=(steps,), out_shape=[jax.ShapeDtypeStru...  9.39 us

profile of v5, /device:TPU:0, one launch (start us, length us, event | category | flops | bytes accessed | tf_op | source)
XLA Modules:
  0.0 183.7 jit_solution(3629496845019535244)
XLA Ops:
  0.6 173.6 %shard_map.120 = (bf16[2,128,1024]{2,1,0:T(8,128)(2,1)}, bf16[2,128,2048]{2,1,0:T(8,128)(2,1)}, bf16[2,128,2048]{2,1,0:T(8,128)(2,1)}, bf16[2,128,1024]{2,1,0:T(...) custom-call(bf16[256,2048]{1,0:T(8,128)(2,1)} %x_t.1, bf16[256,1024]{1,0:T(8,128)(2,1)} %refs_1_.1, ...), custom_call_target="tpu_custom_call" | custom-call | flops 20000000000 | bytes 70000000 | tf_op jit(solution)/shard_map/pallas_call | solution.py:507
  174.3 9.4 %shard_map.121 = (bf16[1024,2048]{1,0:T(8,128)(2,1)}, bf16[1024,2048]{1,0:T(8,128)(2,1)}, bf16[2048,1024]{1,0:T(8,128)(2,1)}, bf16[1024,2048]{1,0:T(8,128)(2,1)}) custom-call(bf16[256,1024]{1,0:T(8,128)(2,1)} %refs_1_.1, bf16[256,1024]{1,0:T(8,128)(2,1)} %refs_1_.1, bf16[256,2048]{1,0:T(8,128)(2,1)} %bitcast.7, bf16[256,1024]{1,0:T(8,128)(2,1)} %bitcast.10, ...), custom_call_target="tpu_custom_call" | custom-call | tf_op jit(solution)/shard_map/pallas_call | solution.py:533
